TPU v7x, 256 devices: a whole 4x4x8 slice. The times are simulated.
256 devices in a mesh: seq: 64 (over z, y, core), head: 4 (over x).
Axes of the slice: x: 4, y: 4, z: 8, core: 2. Of those that a mesh axis runs over, the one named last changes fastest.
Arguments:
- queries: bfloat16 [64, 8192], P('seq', 'head')
- k_cache: bfloat16 [786432, 1024], P('seq', 'head')
- v_cache: bfloat16 [786432, 1024], P('seq', 'head'), may hold values from -6 to 6
- o_weight: bfloat16 [8192, 8192], P('head', 'seq'), may hold values from -0.0625 to 0.0625
- group_size: int32 [6], replicated, may hold values from 2 to 32, as said below
- group_start: int32 [6], replicated, may hold values from 0 to 62, as said below
- cache_len: int32 [6], replicated, may hold values from 1 to 393216, as said below
- owner: int32 [6], replicated, may hold values from 0 to 63, as said below
Outputs:
- projected: bfloat16 [6, 8192], P(None, 'seq')
Inputs may be any that keep to these rules, and one draw needn't show every extreme that they name: `group_size`: each subgroup size is a power of two; one request has 32; the subgroup that ends at seq index 63 has 2. `group_start`: each start is a multiple of its group_size; the subgroups are disjoint and together cover all 64 seq indices. cache_len[r] is at most group_size[r] * 12288, and a request with 32 seq indices has exactly that. owner[r] lies inside request r's subgroup.
All inputs are finite; a program needn't handle non-finite values.
Results may differ from a plain program's by a relative error of at most 0.014.
Values may be sent and summed in bfloat16 or wider, within the bound.
A program may use at most 64 MiB of HBM per device.

v0:
```python
import jax
import jax.numpy as jnp
from jax import lax
from jax.sharding import PartitionSpec as P

HEAD_DIM = 128
BLOCK = 512


NEG = -1e30


def per_device(queries, k_cache, v_cache, o_weight, group_size, group_start, cache_len, owner):
    nseq = lax.axis_size("seq")
    myself = lax.axis_index("seq")
    requests = group_size.shape[0]
    inside_mine = ((myself >= group_start) & (myself < group_start + group_size)).astype(jnp.int32)
    my_start = jnp.sum(group_start * inside_mine)
    my_length = jnp.sum(cache_len * inside_mine)
    my_owner = jnp.sum(owner * inside_mine)
    width = queries.shape[1]
    kv_local = k_cache.shape[1] // HEAD_DIM
    groups = width // k_cache.shape[1]
    slot_count = k_cache.shape[0]
    every_query = lax.all_gather(queries, "seq", axis=0, tiled=True)
    query = lax.dynamic_slice_in_dim(every_query, my_owner, 1, 0)
    query = query.reshape(kv_local, groups, HEAD_DIM)
    scale = HEAD_DIM ** (-0.5)
    live = jnp.clip(my_length - (myself - my_start) * slot_count, 0, slot_count)
    block_count = slot_count // BLOCK

    def score_block(step, carry):
        peak, total, summed = carry
        offset = step * BLOCK
        keys = lax.dynamic_slice_in_dim(k_cache, offset, BLOCK, 0).reshape(
            BLOCK, kv_local, HEAD_DIM
        )
        values = lax.dynamic_slice_in_dim(v_cache, offset, BLOCK, 0).reshape(
            BLOCK, kv_local, HEAD_DIM
        )
        scores = jnp.einsum("agd,sad->ags", query, keys, preferred_element_type=jnp.float32) * scale
        valid = offset + jnp.arange(BLOCK, dtype=jnp.int32) < live
        new_peak = jnp.maximum(peak, jnp.max(jnp.where(valid, scores, NEG), axis=-1))
        expo = jnp.where(valid, jnp.exp(scores - new_peak[..., None]), 0.0)
        shrink = jnp.exp(peak - new_peak)
        total = total * shrink + jnp.sum(expo, axis=-1)
        weights = expo.astype(jnp.bfloat16)
        summed = summed * shrink[..., None] + jnp.einsum(
            "ags,sad->agd", weights, values, preferred_element_type=jnp.float32
        )
        return (new_peak, total, summed)

    start_state = (
        jnp.full((kv_local, groups), NEG, jnp.float32),
        jnp.zeros((kv_local, groups), jnp.float32),
        jnp.zeros((kv_local, groups, HEAD_DIM), jnp.float32),
    )
    peak, total, summed = lax.fori_loop(0, block_count, score_block, start_state)
    all_peak, all_total, all_summed = (
        lax.all_gather(peak[None], "seq", axis=0, tiled=True),
        lax.all_gather(total[None], "seq", axis=0, tiled=True),
        lax.all_gather(summed[None], "seq", axis=0, tiled=True),
    )
    seq_ids = jnp.arange(nseq, dtype=jnp.int32)
    member = (seq_ids[None, :] >= group_start[:, None]) & (
        seq_ids[None, :] < (group_start + group_size)[:, None]
    )
    request_peak = jnp.max(jnp.where(member[:, :, None, None], all_peak[None], NEG), axis=1)
    factor = jnp.where(
        member[:, :, None, None], jnp.exp(all_peak[None] - request_peak[:, None]), 0.0
    )
    request_total = jnp.sum(factor * all_total[None], axis=1)
    request_summed = jnp.einsum(
        "rnag,nagd->ragd", factor, all_summed, precision=lax.Precision.HIGHEST
    )
    attended = (
        (request_summed / request_total[..., None]).reshape(requests, width).astype(jnp.bfloat16)
    )
    partial_out = jnp.dot(attended, o_weight, preferred_element_type=jnp.float32)
    return lax.psum(partial_out, "head").astype(jnp.bfloat16)


def solution(mesh):
    in_specs = (
        P("seq", "head"),
        P("seq", "head"),
        P("seq", "head"),
        P("head", "seq"),
        P(),
        P(),
        P(),
        P(),
    )
    out_specs = P(None, "seq")
    return jax.shard_map(
        per_device, mesh=mesh, in_specs=in_specs, out_specs=out_specs, check_vma=False
    )
```

profile of v0, /device:TPU:1, one launch (start us, length us, event | category | flops | bytes accessed | tf_op | source)
XLA Modules:
  0.0 253.2 jit_solution(1979814559664012118)
XLA Ops:
  0.0 0.7 compare_and_fusion
  0.7 1.4 select_reduce_fusion.2
  4.1 54.9 %all-gather.3 = bf16[64,1,2048]{2,1,0:T(2,128)(2,1)S(1)} all-gather(bf16[1,1,2048]{2,1,0:T(2,128)(2,1)} %bitcast.44), channel_id=1, replica_groups=mesh['seq'=64,'head'=4] {'seq'}, dimensions={0}, use_global_device_ids=true | all-gather | bytes 266240 | tf_op jit(solution)/shard_map/all_gather | solution.py:25
  60.4 49.0 %while.18 = (s32[]{:T(128)}, f32[2,8]{1,0:T(2,128)S(1)}, f32[2,8]{1,0:T(2,128)S(1)}, f32[2,8,128]{2,1,0:T(8,128)S(1)}, s32[]{:T(128)}, /*index=5*/bf16[12288,256...) while((s32[]{:T(128)}, f32[2,8]{1,0:T(2,128)S(1)}, ...), condition=%wide.region_6.7_spmd.clone, body=%wide.region_3.6_spmd.clone.sunk | while | flops 4275287 | bytes 2743483 | solution.py:58
  60.4 1.1 constant_dynamic-slice_fusion.3
  61.6 0.2 select_reduce_fusion.6
  62.4 1.1 constant_dynamic-slice_fusion.3
  63.6 0.2 select_reduce_fusion.6
  64.5 1.1 constant_dynamic-slice_fusion.3
  65.7 0.2 select_reduce_fusion.6
  66.5 1.1 constant_dynamic-slice_fusion.3
  67.7 0.2 select_reduce_fusion.6
  68.5 1.1 constant_dynamic-slice_fusion.3
  69.8 0.2 select_reduce_fusion.6
  70.6 1.1 constant_dynamic-slice_fusion.3
  71.8 0.2 select_reduce_fusion.6
  72.6 1.1 constant_dynamic-slice_fusion.3
  73.9 0.2 select_reduce_fusion.6
  74.7 1.1 constant_dynamic-slice_fusion.3
  75.9 0.2 select_reduce_fusion.6
  76.7 1.1 constant_dynamic-slice_fusion.3
  77.9 0.2 select_reduce_fusion.6
  78.8 1.1 constant_dynamic-slice_fusion.3
  80.0 0.2 select_reduce_fusion.6
  80.8 1.1 constant_dynamic-slice_fusion.3
  82.0 0.2 select_reduce_fusion.6
  82.8 1.1 constant_dynamic-slice_fusion.3
  84.9 1.1 constant_dynamic-slice_fusion.3
  86.1 0.2 select_reduce_fusion.6
  86.9 1.1 constant_dynamic-slice_fusion.3
  89.0 1.1 constant_dynamic-slice_fusion.3
  90.2 0.2 select_reduce_fusion.6
  91.0 1.1 constant_dynamic-slice_fusion.3
  93.0 1.1 constant_dynamic-slice_fusion.3
  95.1 1.1 constant_dynamic-slice_fusion.3
  97.1 1.1 constant_dynamic-slice_fusion.3
  99.2 1.1 constant_dynamic-slice_fusion.3
  100.4 0.2 select_reduce_fusion.6
  101.2 1.1 constant_dynamic-slice_fusion.3
  103.3 1.1 constant_dynamic-slice_fusion.3
  104.5 0.2 select_reduce_fusion.6
  105.3 1.1 constant_dynamic-slice_fusion.3
  107.3 1.1 constant_dynamic-slice_fusion.3
  109.4 42.7 %all-gather.4 = f32[64,2,8]{2,1,0:T(2,128)S(1)} all-gather(f32[1,2,8]{2,1,0:T(2,128)S(1)} %bitcast.41), channel_id=3, replica_groups=mesh['seq'=64,'head'=4] {'seq'}, dimensions={0}, use_global_device_ids=true | all-gather | bytes 4160 | tf_op jit(solution)/shard_map/all_gather | solution.py:60
  152.4 41.5 %all-gather.5 = f32[64,2,8]{2,1,0:T(2,128)S(1)} all-gather(f32[1,2,8]{2,1,0:T(2,128)S(1)} %bitcast.42), channel_id=4, replica_groups=mesh['seq'=64,'head'=4] {'seq'}, dimensions={0}, use_global_device_ids=true | all-gather | bytes 4160 | tf_op jit(solution)/shard_map/all_gather | solution.py:61
  194.1 49.2 %all-gather = f32[128,8,128]{2,1,0:T(8,128)S(1)} all-gather(f32[2,8,128]{2,1,0:T(8,128)S(1)} %get-tuple-element.146), channel_id=2, replica_groups=mesh['seq'=64,'head'=4] {'seq'}, dimensions={0}, use_global_device_ids=true | all-gather | bytes 532480 | tf_op jit(solution)/shard_map/all_gather | solution.py:62
  243.3 0.7 fusion.7
  244.2 9.0 %psum.7 = bf16[6,128]{1,0:T(8,128)(2,1)} all-reduce(f32[6,128]{1,0:T(8,128)S(1)} %fusion.15), channel_id=1, replica_groups=mesh['seq'=64,'head'=4] {'head'}, use_global_device_ids=true, to_apply=%region_9.10 | all-reduce | flops 768 | bytes 4608 | tf_op jit(solution)/shard_map/psum | solution.py:80
  (215 shorter events, 19.7 us)
Async XLA Ops:
  0.0 244.0 %copy-start = (bf16[2048,128]{1,0:T(8,128)(2,1)S(1)}, bf16[2048,128]{1,0:T(8,128)(2,1)}, u32[]{:S(2)}) copy-start(bf16[2048,128]{1,0:T(8,128)(2,1)} %param.13) | copy-start | bytes 1572868
  60.3 91.8 %copy-start.1 = (s32[6]{0:T(128)S(1)}, s32[6]{0:T(128)}, u32[]{:S(2)}) copy-start(s32[6]{0:T(128)} %param.15) | copy-start | bytes 76
where the time goes:
time: 254 us; the launch traced here: 253 us
  blocking collectives  197 us (78%)
  local copies, waits for them, and re-layouts  32.9 us (13%)
  matrix products  11.5 us (5%)
  other arithmetic  7.34 us (3%)
  between operations  3.27 us (1%)
    all_gather x1, blocking collectives, per_device(): every_query = lax.all_gather(queries, 'seq', axis=0, tiled=True)  54.9 us
    all_gather x1, blocking collectives, per_device(): lax.all_gather(summed[None], 'seq', axis=0, tiled=True)  49.2 us
    all_gather x1, blocking collectives, per_device(): lax.all_gather(peak[None], 'seq', axis=0, tiled=True)  42.7 us
    all_gather x1, blocking collectives, per_device(): lax.all_gather(total[None], 'seq', axis=0, tiled=True)  41.5 us
    dynamic_slice x48, local copies, waits for them, and re-layouts, score_block(): lax.dynamic_slice_in_dim(v_cache, offset, BLOCK, 0)  29.3 us
    psum x1, blocking collectives, per_device(): return lax.psum(partial_out, 'head').astype(jnp.bfloat16)  9.04 us
    dot_general x24, matrix products, score_block(): jnp.einsum('agd,sad->ags', query, keys, preferred_element_type=jnp.float32)  5.49 us

commit v1 on v0

v1 whole, which is shorter than its diff:
```python
import functools

import jax
import jax.numpy as jnp
from jax import lax
from jax.experimental import pallas as pl
from jax.experimental.pallas import tpu as pltpu
from jax.sharding import PartitionSpec as P

HEAD_DIM = 128
MESH = pl.DeviceIdType.MESH
LOG2E = 1.4426950408889634
SCALE = HEAD_DIM ** (-0.5)
EXPO = SCALE * LOG2E
NEG = -1e30 / SCALE
BLOCK = 32
PARTS = 4
CHUNK = 1024


def attend(query, k_vmem, v_vmem, live, slots):
    zero = jnp.zeros((8, HEAD_DIM), jnp.bfloat16)
    wide = jnp.concatenate(
        [
            jnp.concatenate([query[:8], zero], axis=1),
            jnp.concatenate([zero, query[8:]], axis=1),
        ],
        axis=0,
    )
    lane = lax.broadcasted_iota(jnp.int32, (16, CHUNK), 1)
    per_part = slots // PARTS
    found = []
    for part in range(PARTS):
        scores = []
        for first in range(part * per_part, (part + 1) * per_part, CHUNK):
            keys = k_vmem[first : first + CHUNK, :]
            score = lax.dot_general(
                wide, keys, (((1,), (1,)), ((), ())), preferred_element_type=jnp.float32
            )
            scores.append(jnp.where(lane < live - first, score, NEG))
        peak = functools.reduce(jnp.maximum, scores)
        peak = jnp.max(peak, axis=1, keepdims=True)
        total = jnp.zeros((16, CHUNK), jnp.float32)
        summed = jnp.zeros((16, 2 * HEAD_DIM), jnp.float32)
        for step, score in enumerate(scores):
            first = part * per_part + step * CHUNK
            expo = jnp.exp2((score - peak) * EXPO)
            total = total + expo
            summed = summed + jnp.dot(
                expo.astype(jnp.bfloat16),
                v_vmem[first : first + CHUNK, :],
                preferred_element_type=jnp.float32,
            )
        found.append((peak, jnp.sum(total, axis=1, keepdims=True), summed))
    top = functools.reduce(jnp.maximum, [peak for peak, _, _ in found])
    total = jnp.zeros((16, 1), jnp.float32)
    summed = jnp.zeros((16, 2 * HEAD_DIM), jnp.float32)
    for peak, part_total, part_summed in found:
        shrink = jnp.exp2((peak - top) * EXPO)
        total = total + part_total * shrink
        summed = summed + part_summed * shrink
    return top, total, summed


def kernel(
    q_ref,
    k_hbm,
    v_hbm,
    w_hbm,
    size_ref,
    start_ref,
    length_ref,
    owner_ref,
    out_ref,
    k_vmem,
    v_vmem,
    w_vmem,
    q_all,
    swap_out,
    swap_in,
    gathered,
    product,
    terms,
    load_sem,
    send_sem,
    recv_sem,
):
    me = lax.axis_index("seq")
    x = lax.axis_index("head")
    slots = k_hbm.shape[0]
    requests = size_ref.shape[0]
    base = (me // BLOCK) * BLOCK
    off = me - base
    core = me % 2
    chip = me // 2
    other = me + 1 - 2 * core
    chips = lax.axis_size("seq") // 2
    heads = lax.axis_size("head")
    half = w_hbm.shape[0] // 2

    loads = []
    for part in range(PARTS):
        rows = pl.ds(part * (slots // PARTS), slots // PARTS)
        loads.append(
            pltpu.make_async_copy(k_hbm.at[rows], k_vmem.at[rows], load_sem.at[part])
        )
    for part in range(PARTS):
        rows = pl.ds(part * (slots // PARTS), slots // PARTS)
        loads.append(
            pltpu.make_async_copy(v_hbm.at[rows], v_vmem.at[rows], load_sem.at[PARTS + part])
        )
    mine = pl.ds(pl.multiple_of(core * half, half), half)
    theirs = pl.ds(pl.multiple_of((1 - core) * half, half), half)
    loads.append(pltpu.make_async_copy(w_hbm.at[mine], w_vmem.at[0], load_sem.at[2 * PARTS]))
    for load in loads:
        load.start()

    def in_block(step):
        return base + (off + step) % BLOCK

    def far_chip(step):
        return ((chip + step) % chips) * 2 + core

    barrier = pltpu.get_barrier_semaphore()

    @pl.loop(1, BLOCK)
    def _(step):
        pl.semaphore_signal(barrier, 1, device_id={"seq": in_block(step)}, device_id_type=MESH)

    other_half = ((me // BLOCK + 1) % 2) * BLOCK + core

    @pl.loop(0, BLOCK // 2)
    def _(step):
        pl.semaphore_signal(
            barrier, 1, device_id={"seq": other_half + 2 * step}, device_id_type=MESH
        )

    for step in range(1, heads):
        across = (x + step) % heads
        for seq in (me, other):
            pl.semaphore_signal(
                barrier, 1, device_id={"seq": seq, "head": across}, device_id_type=MESH
            )

    query = q_ref[...].astype(jnp.float32)
    rows = [query[:, h * HEAD_DIM : (h + 1) * HEAD_DIM] for h in range(16)]
    q_all[off] = jnp.concatenate(rows, axis=0).astype(jnp.bfloat16)
    pl.semaphore_wait(barrier, (BLOCK - 1) + BLOCK // 2 + 2 * (heads - 1))

    @pl.loop(1, BLOCK)
    def _(step):
        pltpu.make_async_remote_copy(
            src_ref=q_all.at[off],
            dst_ref=q_all.at[off],
            send_sem=send_sem.at[0],
            recv_sem=recv_sem.at[0],
            device_id={"seq": in_block(step)},
            device_id_type=MESH,
        ).start()

    weight_copy = pltpu.make_async_remote_copy(
        src_ref=w_hbm.at[theirs],
        dst_ref=w_vmem.at[1],
        send_sem=send_sem.at[1],
        recv_sem=recv_sem.at[1],
        device_id={"seq": other},
        device_id_type=MESH,
    )
    weight_copy.start()

    my_start = jnp.int32(0)
    my_length = jnp.int32(0)
    my_owner = jnp.int32(0)
    for r in range(requests):
        inside = (me >= start_ref[r]) & (me < start_ref[r] + size_ref[r])
        my_start = my_start + jnp.where(inside, start_ref[r], 0)
        my_length = my_length + jnp.where(inside, length_ref[r], 0)
        my_owner = my_owner + jnp.where(inside, owner_ref[r], 0)
    live = my_length - (me - my_start) * slots

    for load in loads:
        load.wait()
    queries_in = q_all.at[pl.ds(0, BLOCK - 1)]
    queries_copy = pltpu.make_async_remote_copy(
        src_ref=queries_in,
        dst_ref=queries_in,
        send_sem=send_sem.at[0],
        recv_sem=recv_sem.at[0],
        device_id={"seq": other},
        device_id_type=MESH,
    )
    queries_copy.wait_recv()
    top, total, summed = attend(q_all[lax.rem(my_owner, BLOCK)], k_vmem, v_vmem, live, slots)

    first = core == 0
    low = (
        summed[:8, :HEAD_DIM],
        jnp.broadcast_to(top[:8], (8, HEAD_DIM)),
        jnp.broadcast_to(total[:8], (8, HEAD_DIM)),
    )
    high = (
        summed[8:, HEAD_DIM:],
        jnp.broadcast_to(top[8:], (8, HEAD_DIM)),
        jnp.broadcast_to(total[8:], (8, HEAD_DIM)),
    )
    for i in range(3):
        swap_out[8 * i : 8 * i + 8, :] = jnp.where(first, high[i], low[i])
    swap = pltpu.make_async_remote_copy(
        src_ref=swap_out,
        dst_ref=swap_in,
        send_sem=send_sem.at[2],
        recv_sem=recv_sem.at[2],
        device_id={"seq": other},
        device_id_type=MESH,
    )
    swap.start()
    summed, top, total = (jnp.where(first, low[i], high[i]) for i in range(3))
    swap.wait_recv()
    their_top = swap_in[8:16, :]
    new_top = jnp.maximum(top, their_top)
    shrink = jnp.exp2((top - new_top) * EXPO)
    their_shrink = jnp.exp2((their_top - new_top) * EXPO)
    gathered[chip, 0:8, :] = summed * shrink + swap_in[0:8, :] * their_shrink
    total = total * shrink + swap_in[16:24, :] * their_shrink
    lane = lax.broadcasted_iota(jnp.int32, (8, HEAD_DIM), 1)
    row = lax.broadcasted_iota(jnp.int32, (8, HEAD_DIM), 0)
    facts = jnp.where(lane == row, new_top, 0.0) + jnp.where(lane == row + 8, total, 0.0)
    gathered[chip, 8:9, :] = jnp.sum(facts, axis=0, keepdims=True)

    @pl.loop(1, chips)
    def _(step):
        pltpu.make_async_remote_copy(
            src_ref=gathered.at[chip, pl.ds(0, 9)],
            dst_ref=gathered.at[chip, pl.ds(0, 9)],
            send_sem=send_sem.at[3],
            recv_sem=recv_sem.at[3],
            device_id={"seq": far_chip(step)},
            device_id_type=MESH,
        ).start()

    starts = jnp.zeros((8, chips), jnp.int32)
    ends = jnp.zeros((8, chips), jnp.int32)
    request = lax.broadcasted_iota(jnp.int32, (8, chips), 0)
    seq_of = 2 * lax.broadcasted_iota(jnp.int32, (8, chips), 1)
    for r in range(requests):
        starts = jnp.where(request == r, start_ref[r], starts)
        ends = jnp.where(request == r, start_ref[r] + size_ref[r], ends)
    member = ((seq_of >= starts) & (seq_of < ends)).astype(jnp.float32).astype(jnp.bfloat16)
    seq_down = 2 * lax.broadcasted_iota(jnp.int32, (chips, HEAD_DIM), 0)
    serves = [
        (seq_down >= start_ref[r]) & (seq_down < start_ref[r] + size_ref[r])
        for r in range(requests)
    ]

    gathered_in = gathered.at[pl.ds(0, chips - 1), pl.ds(0, 9)]
    gathered_copy = pltpu.make_async_remote_copy(
        src_ref=gathered_in,
        dst_ref=gathered_in,
        send_sem=send_sem.at[3],
        recv_sem=recv_sem.at[3],
        device_id={"seq": other},
        device_id_type=MESH,
    )
    gathered_copy.wait_recv()

    facts = gathered[:, 8, :]
    totals = pltpu.roll(facts, HEAD_DIM - 8, 1)
    tops = jnp.zeros((chips, HEAD_DIM), jnp.float32)
    for r in range(requests):
        top = jnp.max(jnp.where(serves[r], facts, NEG), axis=0, keepdims=True)
        tops = jnp.where(serves[r], top, tops)
    lane = lax.broadcasted_iota(jnp.int32, (chips, HEAD_DIM), 1)
    factor = jnp.exp2(jnp.where(lane < 8, (facts - tops) * EXPO, 0.0))
    scaled = factor * totals
    sums = jnp.ones((chips, HEAD_DIM), jnp.float32)
    for r in range(requests):
        total = jnp.sum(jnp.where(serves[r], scaled, 0.0), axis=0, keepdims=True)
        sums = jnp.where(serves[r], total, sums)
    factor = factor / sums
    pieces = [gathered[:, h, :] * factor[:, h : h + 1] for h in range(8)]
    weighted = jnp.concatenate(pieces, axis=1).astype(jnp.bfloat16)
    attended = jnp.dot(member, weighted, preferred_element_type=jnp.float32).astype(jnp.bfloat16)

    weight_copy.wait_recv()
    slot = 2 * x + core
    product[0] = jnp.dot(attended, w_vmem[1], preferred_element_type=jnp.float32)
    ours = jnp.dot(attended, w_vmem[0], preferred_element_type=jnp.float32)
    product[1] = ours
    terms[slot] = ours

    def final(which, seq, across):
        return pltpu.make_async_remote_copy(
            src_ref=product.at[which],
            dst_ref=terms.at[slot],
            send_sem=send_sem.at[4],
            recv_sem=recv_sem.at[4],
            device_id={"seq": seq, "head": across},
            device_id_type=MESH,
        )

    for step in (2, 1, 3):
        final(0, other, (x + step) % heads).start()
        final(1, me, (x + step) % heads).start()
    final(0, other, x).start()

    terms_in = terms.at[pl.ds(0, 2 * heads - 1)]
    terms_copy = pltpu.make_async_remote_copy(
        src_ref=terms_in,
        dst_ref=terms_in,
        send_sem=send_sem.at[4],
        recv_sem=recv_sem.at[4],
        device_id={"seq": other},
        device_id_type=MESH,
    )
    terms_copy.wait_recv()
    out = terms[0]
    for i in range(1, 2 * heads):
        out = out + terms[i]
    out_ref[...] = out[:requests].astype(jnp.bfloat16)
    queries_copy.wait_send()
    weight_copy.wait_send()
    swap.wait_send()
    gathered_copy.wait_send()
    terms_copy.wait_send()


def per_device(queries, k_cache, v_cache, o_weight, group_size, group_start, cache_len, owner):
    requests = group_size.shape[0]
    slots, width = k_cache.shape
    rows, columns = o_weight.shape
    chips = lax.axis_size("seq") // 2
    heads = lax.axis_size("head")
    hbm = pl.BlockSpec(memory_space=pl.ANY)
    vmem = pl.BlockSpec(memory_space=pltpu.VMEM)
    smem = pl.BlockSpec(memory_space=pltpu.SMEM)
    return pl.pallas_call(
        kernel,
        out_shape=jax.ShapeDtypeStruct((requests, columns), jnp.bfloat16),
        in_specs=[vmem, hbm, hbm, hbm, smem, smem, smem, smem],
        out_specs=vmem,
        scratch_shapes=[
            pltpu.VMEM((slots, width), jnp.bfloat16),
            pltpu.VMEM((slots, width), jnp.bfloat16),
            pltpu.VMEM((2, rows // 2, columns), jnp.bfloat16),
            pltpu.VMEM((BLOCK, 16, HEAD_DIM), jnp.bfloat16),
            pltpu.VMEM((24, HEAD_DIM), jnp.float32),
            pltpu.VMEM((24, HEAD_DIM), jnp.float32),
            pltpu.VMEM((chips, 16, HEAD_DIM), jnp.float32),
            pltpu.VMEM((2, 8, columns), jnp.float32),
            pltpu.VMEM((2 * heads, 8, columns), jnp.float32),
            pltpu.SemaphoreType.DMA((2 * PARTS + 1,)),
            pltpu.SemaphoreType.DMA((5,)),
            pltpu.SemaphoreType.DMA((5,)),
        ],
        compiler_params=pltpu.CompilerParams(
            collective_id=0, has_side_effects=True, vmem_limit_bytes=56 * 1024 * 1024
        ),
    )(queries, k_cache, v_cache, o_weight, group_size, group_start, cache_len, owner)


def solution(mesh):
    in_specs = (
        P("seq", "head"),
        P("seq", "head"),
        P("seq", "head"),
        P("head", "seq"),
        P(),
        P(),
        P(),
        P(),
    )
    out_specs = P(None, "seq")
    return jax.shard_map(
        per_device, mesh=mesh, in_specs=in_specs, out_specs=out_specs, check_vma=False
    )
```

time: 254 us -> 36 us (0.14)
  blocking collectives: 197 us -> 0 us
  Pallas kernels: 0 us -> 34.6 us
  local copies, waits for them, and re-layouts: 32.9 us -> 1.26 us
  matrix products: 11.5 us -> 0 us
  other arithmetic: 7.34 us -> 0 us
  between operations: 3.27 us -> 0.01 us
    all_gather x4 -> x0, blocking collectives: 188 us -> none  [the longest x1 54.9 us: per_device(): every_query = lax.all_gather(queries, 'seq', axis=0, tiled=True)]
    pallas_call x0 -> x1, Pallas kernels: none -> 34.6 us  [per_device(): pl.pallas_call(kernel, out_shape=jax.ShapeDtypeStruct((requests, columns)...]
    dynamic_slice x73 -> x0, local copies, waits for them, and re-layouts: 32.7 us -> none  [the longest x48 29.3 us: score_block(): lax.dynamic_slice_in_dim(v_cache, offset, BLOCK, 0)]
    dot_general x50 -> x0, matrix products: 11.5 us -> none  [the longest x24 5.49 us: score_block(): jnp.einsum('agd,sad->ags', query, keys, preferred_element_type=jnp.float32)]
    psum x1 -> x0, blocking collectives: 9.04 us -> none  [per_device(): return lax.psum(partial_out, 'head').astype(jnp.bfloat16)]
    reduce_sum x26 -> x0, other arithmetic: 5.68 us -> none  [the longest x24 4.09 us: score_block(): total = total * shrink + jnp.sum(expo, axis=-1)]
where the time goes in v1:
time: 36 us; the launch traced here: 35.8 us
  Pallas kernels  34.6 us (96%)
  local copies, waits for them, and re-layouts  1.26 us (4%)
    pallas_call x1, Pallas kernels, per_device(): pl.pallas_call(kernel, out_shape=jax.ShapeDtypeStruct((requests, columns)...  34.6 us
    unnamed x1, local copies, waits for them, and re-layouts  1.26 us

profile of v1, /device:TPU:1, one launch (start us, length us, event | category | flops | bytes accessed | tf_op | source)
XLA Modules:
  0.0 35.8 jit_solution(15234753044013721675)
XLA Ops:
  0.0 34.6 %shard_map.82 = bf16[6,128]{1,0:T(8,128)(2,1)} custom-call(bf16[1,2048]{1,0:T(2,128)(2,1)} %q_ref.1, bf16[12288,256]{1,0:T(8,128)(2,1)} %k_hbm.1, bf16[12288,256]{1,0:T(8,128)(2,1)} %v_hbm.1, bf16[2048,128]{1,0:T(8,128)(2,1)} %w_hbm.1, s32[6]{0:T(128)} %size_ref.1, s32[6]{0:T(128)} %start_ref.1, s32[6]{0:T(128)} %length_ref.1, s32[6]{0:T(128)} %owner_ref.1), custom_call_target="tpu_custom_call" | custom-call | tf_op jit(solution)/shard_map/pallas_call | solution.py:336
  34.6 1.3 %copy.10 = bf16[6,128]{1,0:T(8,128)(2,1)} copy(bf16[6,128]{1,0:T(8,128)(2,1)} %shard_map.82) | data formatting | bytes 3072

commit v2 on v1

--- a/solution.py
+++ b/solution.py
@@ -14,34 +14,29 @@
 EXPO = SCALE * LOG2E
 NEG = -1e30 / SCALE
 BLOCK = 32
+WIDTH = 4
 PARTS = 4
 CHUNK = 1024
-
-
-def attend(query, k_vmem, v_vmem, live, slots):
-    zero = jnp.zeros((8, HEAD_DIM), jnp.bfloat16)
-    wide = jnp.concatenate(
-        [
-            jnp.concatenate([query[:8], zero], axis=1),
-            jnp.concatenate([zero, query[8:]], axis=1),
-        ],
-        axis=0,
-    )
-    lane = lax.broadcasted_iota(jnp.int32, (16, CHUNK), 1)
+TURN = 256
+
+
+def attend(query, k_turned, v_vmem, live, slots):
+    lane = lax.broadcasted_iota(jnp.int32, (8, CHUNK), 1)
     per_part = slots // PARTS
-    found = []
-    for part in range(PARTS):
+
+    def score_part(part):
         scores = []
         for first in range(part * per_part, (part + 1) * per_part, CHUNK):
-            keys = k_vmem[first : first + CHUNK, :]
-            score = lax.dot_general(
-                wide, keys, (((1,), (1,)), ((), ())), preferred_element_type=jnp.float32
-            )
+            keys = k_turned[:, first : first + CHUNK]
+            score = jnp.dot(query, keys, preferred_element_type=jnp.float32)
             scores.append(jnp.where(lane < live - first, score, NEG))
+        return scores
+
+    def value_part(part, scores):
         peak = functools.reduce(jnp.maximum, scores)
         peak = jnp.max(peak, axis=1, keepdims=True)
-        total = jnp.zeros((16, CHUNK), jnp.float32)
-        summed = jnp.zeros((16, 2 * HEAD_DIM), jnp.float32)
+        total = jnp.zeros((8, CHUNK), jnp.float32)
+        summed = jnp.zeros((8, HEAD_DIM), jnp.float32)
         for step, score in enumerate(scores):
             first = part * per_part + step * CHUNK
             expo = jnp.exp2((score - peak) * EXPO)
@@ -51,28 +46,49 @@
                 v_vmem[first : first + CHUNK, :],
                 preferred_element_type=jnp.float32,
             )
-        found.append((peak, jnp.sum(total, axis=1, keepdims=True), summed))
+        return peak, jnp.sum(total, axis=1, keepdims=True), summed
+
+    found = []
+    scores = score_part(0)
+    for part in range(1, PARTS):
+        following = score_part(part)
+        found.append(value_part(part - 1, scores))
+        scores = following
+    found.append(value_part(PARTS - 1, scores))
     top = functools.reduce(jnp.maximum, [peak for peak, _, _ in found])
-    total = jnp.zeros((16, 1), jnp.float32)
-    summed = jnp.zeros((16, 2 * HEAD_DIM), jnp.float32)
+    total = jnp.zeros((8, 1), jnp.float32)
+    summed = jnp.zeros((8, HEAD_DIM), jnp.float32)
     for peak, part_total, part_summed in found:
         shrink = jnp.exp2((peak - top) * EXPO)
         total = total + part_total * shrink
         summed = summed + part_summed * shrink
-    return top, total, summed
+    shape = (8, HEAD_DIM)
+    return jnp.broadcast_to(top, shape), jnp.broadcast_to(total, shape), summed
+
+
+def far_first(length, width):
+    steps = [(z, y) for z in range(length) for y in range(width)]
+    steps.sort(key=lambda s: -(min(s[0], length - s[0]) + min(s[1], width - s[1])))
+    return steps
 
 
 def kernel(
-    q_ref,
+    q_hbm,
     k_hbm,
     v_hbm,
     w_hbm,
+    size_hbm,
+    start_hbm,
+    length_hbm,
+    owner_hbm,
+    out_ref,
+    q_ref,
     size_ref,
     start_ref,
     length_ref,
     owner_ref,
-    out_ref,
     k_vmem,
+    k_turned,
     v_vmem,
     w_vmem,
     q_all,
@@ -98,43 +114,56 @@
     heads = lax.axis_size("head")
     half = w_hbm.shape[0] // 2
 
+    columns = [
+        pl.ds(pl.multiple_of((1 - core) * HEAD_DIM, HEAD_DIM), HEAD_DIM),
+        pl.ds(pl.multiple_of(core * HEAD_DIM, HEAD_DIM), HEAD_DIM),
+    ]
     loads = []
-    for part in range(PARTS):
-        rows = pl.ds(part * (slots // PARTS), slots // PARTS)
-        loads.append(
-            pltpu.make_async_copy(k_hbm.at[rows], k_vmem.at[rows], load_sem.at[part])
-        )
-    for part in range(PARTS):
-        rows = pl.ds(part * (slots // PARTS), slots // PARTS)
-        loads.append(
-            pltpu.make_async_copy(v_hbm.at[rows], v_vmem.at[rows], load_sem.at[PARTS + part])
-        )
+    for hbm, vmem in ((k_hbm, k_vmem), (v_hbm, v_vmem)):
+        for turn in range(2):
+            loads.append(
+                pltpu.make_async_copy(
+                    hbm.at[:, columns[turn]], vmem.at[turn], load_sem.at[len(loads)]
+                )
+            )
     mine = pl.ds(pl.multiple_of(core * half, half), half)
     theirs = pl.ds(pl.multiple_of((1 - core) * half, half), half)
-    loads.append(pltpu.make_async_copy(w_hbm.at[mine], w_vmem.at[0], load_sem.at[2 * PARTS]))
-    for load in loads:
+    loads.append(pltpu.make_async_copy(w_hbm.at[mine], w_vmem.at[0], load_sem.at[4]))
+    facts_in = [pltpu.make_async_copy(a, b, load_sem.at[5 + i]) for i, (a, b) in enumerate(((size_hbm, size_ref), (start_hbm, start_ref), (length_hbm, length_ref), (owner_hbm, owner_ref)))]
+    query_in = pltpu.make_async_copy(q_hbm, q_ref, load_sem.at[9])
+    query_in.start()
+
+    z, y = chip // WIDTH, chip % WIDTH
+    length = chips // WIDTH
+    quarter = BLOCK // (2 * WIDTH)
+    z_first = (z // quarter) * quarter
+
+    def block_peers():
+        for dz, dy in far_first(quarter, WIDTH):
+            there = 2 * ((z_first + (z + dz) % quarter) * WIDTH + (y + dy) % WIDTH)
+            yield there + 1 - core
+            if (dz, dy) != (0, 0):
+                yield there + core
+
+    def plane_peers():
+        for dz, dy in far_first(length, WIDTH):
+            if (dz, dy) != (0, 0):
+                yield 2 * (((z + dz) % length) * WIDTH + (y + dy) % WIDTH) + core
+
+    other_half = ((me // BLOCK + 1) % 2) * quarter
+
+    def other_half_peers():
+        for dz, dy in far_first(quarter, WIDTH):
+            yield 2 * ((other_half + (z + dz) % quarter) * WIDTH + (y + dy) % WIDTH) + core
+
+    barrier = pltpu.get_barrier_semaphore()
+
+    for peer in block_peers():
+        pl.semaphore_signal(barrier, 1, device_id={"seq": peer}, device_id_type=MESH)
+    for load in facts_in + loads:
         load.start()
-
-    def in_block(step):
-        return base + (off + step) % BLOCK
-
-    def far_chip(step):
-        return ((chip + step) % chips) * 2 + core
-
-    barrier = pltpu.get_barrier_semaphore()
-
-    @pl.loop(1, BLOCK)
-    def _(step):
-        pl.semaphore_signal(barrier, 1, device_id={"seq": in_block(step)}, device_id_type=MESH)
-
-    other_half = ((me // BLOCK + 1) % 2) * BLOCK + core
-
-    @pl.loop(0, BLOCK // 2)
-    def _(step):
-        pl.semaphore_signal(
-            barrier, 1, device_id={"seq": other_half + 2 * step}, device_id_type=MESH
-        )
-
+    for peer in other_half_peers():
+        pl.semaphore_signal(barrier, 1, device_id={"seq": peer}, device_id_type=MESH)
     for step in range(1, heads):
         across = (x + step) % heads
         for seq in (me, other):
@@ -142,19 +171,19 @@
                 barrier, 1, device_id={"seq": seq, "head": across}, device_id_type=MESH
             )
 
+    query_in.wait()
     query = q_ref[...].astype(jnp.float32)
     rows = [query[:, h * HEAD_DIM : (h + 1) * HEAD_DIM] for h in range(16)]
     q_all[off] = jnp.concatenate(rows, axis=0).astype(jnp.bfloat16)
     pl.semaphore_wait(barrier, (BLOCK - 1) + BLOCK // 2 + 2 * (heads - 1))
 
-    @pl.loop(1, BLOCK)
-    def _(step):
+    for peer in block_peers():
         pltpu.make_async_remote_copy(
             src_ref=q_all.at[off],
             dst_ref=q_all.at[off],
             send_sem=send_sem.at[0],
             recv_sem=recv_sem.at[0],
-            device_id={"seq": in_block(step)},
+            device_id={"seq": peer},
             device_id_type=MESH,
         ).start()
 
@@ -166,8 +195,10 @@
         device_id={"seq": other},
         device_id_type=MESH,
     )
+
     weight_copy.start()
-
+    for load in facts_in:
+        load.wait()
     my_start = jnp.int32(0)
     my_length = jnp.int32(0)
     my_owner = jnp.int32(0)
@@ -178,7 +209,12 @@
         my_owner = my_owner + jnp.where(inside, owner_ref[r], 0)
     live = my_length - (me - my_start) * slots
 
-    for load in loads:
+    for turn in range(2):
+        loads[turn].wait()
+        for first in range(0, slots, TURN):
+            rows = slice(first, first + TURN)
+            k_turned[turn, :, rows] = k_vmem[turn, rows, :].T
+    for load in loads[2:]:
         load.wait()
     queries_in = q_all.at[pl.ds(0, BLOCK - 1)]
     queries_copy = pltpu.make_async_remote_copy(
@@ -190,21 +226,14 @@
         device_id_type=MESH,
     )
     queries_copy.wait_recv()
-    top, total, summed = attend(q_all[lax.rem(my_owner, BLOCK)], k_vmem, v_vmem, live, slots)
-
+    query = q_all[lax.rem(my_owner, BLOCK)]
     first = core == 0
-    low = (
-        summed[:8, :HEAD_DIM],
-        jnp.broadcast_to(top[:8], (8, HEAD_DIM)),
-        jnp.broadcast_to(total[:8], (8, HEAD_DIM)),
-    )
-    high = (
-        summed[8:, HEAD_DIM:],
-        jnp.broadcast_to(top[8:], (8, HEAD_DIM)),
-        jnp.broadcast_to(total[8:], (8, HEAD_DIM)),
+
+    theirs = attend(
+        jnp.where(first, query[8:], query[:8]), k_turned.at[0], v_vmem.at[0], live, slots
     )
     for i in range(3):
-        swap_out[8 * i : 8 * i + 8, :] = jnp.where(first, high[i], low[i])
+        swap_out[8 * i : 8 * i + 8, :] = theirs[i]
     swap = pltpu.make_async_remote_copy(
         src_ref=swap_out,
         dst_ref=swap_in,
@@ -214,27 +243,28 @@
         device_id_type=MESH,
     )
     swap.start()
-    summed, top, total = (jnp.where(first, low[i], high[i]) for i in range(3))
+    top, total, summed = attend(
+        jnp.where(first, query[:8], query[8:]), k_turned.at[1], v_vmem.at[1], live, slots
+    )
     swap.wait_recv()
-    their_top = swap_in[8:16, :]
+    their_top = swap_in[0:8, :]
     new_top = jnp.maximum(top, their_top)
     shrink = jnp.exp2((top - new_top) * EXPO)
     their_shrink = jnp.exp2((their_top - new_top) * EXPO)
-    gathered[chip, 0:8, :] = summed * shrink + swap_in[0:8, :] * their_shrink
-    total = total * shrink + swap_in[16:24, :] * their_shrink
+    gathered[chip, 0:8, :] = summed * shrink + swap_in[16:24, :] * their_shrink
+    total = total * shrink + swap_in[8:16, :] * their_shrink
     lane = lax.broadcasted_iota(jnp.int32, (8, HEAD_DIM), 1)
     row = lax.broadcasted_iota(jnp.int32, (8, HEAD_DIM), 0)
     facts = jnp.where(lane == row, new_top, 0.0) + jnp.where(lane == row + 8, total, 0.0)
     gathered[chip, 8:9, :] = jnp.sum(facts, axis=0, keepdims=True)
 
-    @pl.loop(1, chips)
-    def _(step):
+    for peer in plane_peers():
         pltpu.make_async_remote_copy(
             src_ref=gathered.at[chip, pl.ds(0, 9)],
             dst_ref=gathered.at[chip, pl.ds(0, 9)],
             send_sem=send_sem.at[3],
             recv_sem=recv_sem.at[3],
-            device_id={"seq": far_chip(step)},
+            device_id={"seq": peer},
             device_id_type=MESH,
         ).start()
 
@@ -312,15 +342,15 @@
         device_id={"seq": other},
         device_id_type=MESH,
     )
+    queries_copy.wait_send()
+    weight_copy.wait_send()
+    swap.wait_send()
+    gathered_copy.wait_send()
     terms_copy.wait_recv()
     out = terms[0]
     for i in range(1, 2 * heads):
         out = out + terms[i]
     out_ref[...] = out[:requests].astype(jnp.bfloat16)
-    queries_copy.wait_send()
-    weight_copy.wait_send()
-    swap.wait_send()
-    gathered_copy.wait_send()
     terms_copy.wait_send()
 
 
@@ -336,11 +366,17 @@
     return pl.pallas_call(
         kernel,
         out_shape=jax.ShapeDtypeStruct((requests, columns), jnp.bfloat16),
-        in_specs=[vmem, hbm, hbm, hbm, smem, smem, smem, smem],
+        in_specs=[hbm, hbm, hbm, hbm, hbm, hbm, hbm, hbm],
         out_specs=vmem,
         scratch_shapes=[
-            pltpu.VMEM((slots, width), jnp.bfloat16),
-            pltpu.VMEM((slots, width), jnp.bfloat16),
+            pltpu.VMEM(queries.shape, jnp.bfloat16),
+            pltpu.SMEM((requests,), jnp.int32),
+            pltpu.SMEM((requests,), jnp.int32),
+            pltpu.SMEM((requests,), jnp.int32),
+            pltpu.SMEM((requests,), jnp.int32),
+            pltpu.VMEM((2, slots, width // 2), jnp.bfloat16),
+            pltpu.VMEM((2, width // 2, slots), jnp.bfloat16),
+            pltpu.VMEM((2, slots, width // 2), jnp.bfloat16),
             pltpu.VMEM((2, rows // 2, columns), jnp.bfloat16),
             pltpu.VMEM((BLOCK, 16, HEAD_DIM), jnp.bfloat16),
             pltpu.VMEM((24, HEAD_DIM), jnp.float32),
@@ -348,7 +384,7 @@
             pltpu.VMEM((chips, 16, HEAD_DIM), jnp.float32),
             pltpu.VMEM((2, 8, columns), jnp.float32),
             pltpu.VMEM((2 * heads, 8, columns), jnp.float32),
-            pltpu.SemaphoreType.DMA((2 * PARTS + 1,)),
+            pltpu.SemaphoreType.DMA((10,)),
             pltpu.SemaphoreType.DMA((5,)),
             pltpu.SemaphoreType.DMA((5,)),
         ],

time: 36 us -> 31.8 us (0.88)
  Pallas kernels: 34.6 us -> 30.4 us
    pallas_call x1, Pallas kernels: 34.6 us -> 30.4 us  [per_device(): pl.pallas_call(kernel, out_shape=jax.ShapeDtypeStruct((requests, columns)...]
where the time goes in v2:
time: 31.8 us; the launch traced here: 31.6 us
  Pallas kernels  30.4 us (96%)
  local copies, waits for them, and re-layouts  1.26 us (4%)
    pallas_call x1, Pallas kernels, per_device(): pl.pallas_call(kernel, out_shape=jax.ShapeDtypeStruct((requests, columns)...  30.4 us
    unnamed x1, local copies, waits for them, and re-layouts  1.26 us

profile of v2, /device:TPU:1, one launch (start us, length us, event | category | flops | bytes accessed | tf_op | source)
XLA Modules:
  0.0 31.6 jit_solution(7842830532538195233)
XLA Ops:
  0.0 30.4 %shard_map.82 = bf16[6,128]{1,0:T(8,128)(2,1)} custom-call(bf16[1,2048]{1,0:T(2,128)(2,1)} %q_hbm.1, bf16[12288,256]{1,0:T(8,128)(2,1)} %k_hbm.1, bf16[12288,256]{1,0:T(8,128)(2,1)} %v_hbm.1, bf16[2048,128]{1,0:T(8,128)(2,1)} %w_hbm.1, s32[6]{0:T(128)} %size_hbm.1, s32[6]{0:T(128)} %start_hbm.1, s32[6]{0:T(128)} %length_hbm.1, s32[6]{0:T(128)} %owner_hbm.1), custom_call_target="tpu_custom_call" | custom-call | tf_op jit(solution)/shard_map/pallas_call | solution.py:366
  30.4 1.3 %copy.10 = bf16[6,128]{1,0:T(8,128)(2,1)} copy(bf16[6,128]{1,0:T(8,128)(2,1)} %shard_map.82) | data formatting | bytes 3072

commit v3 on v2

--- a/solution.py
+++ b/solution.py
@@ -81,7 +81,7 @@
     start_hbm,
     length_hbm,
     owner_hbm,
-    out_ref,
+    terms,
     q_ref,
     size_ref,
     start_ref,
@@ -96,10 +96,10 @@
     swap_in,
     gathered,
     product,
-    terms,
     load_sem,
     send_sem,
     recv_sem,
+    late_sem,
 ):
     me = lax.axis_index("seq")
     x = lax.axis_index("head")
@@ -138,6 +138,8 @@
     quarter = BLOCK // (2 * WIDTH)
     z_first = (z // quarter) * quarter
 
+    early = me < BLOCK
+
     def block_peers():
         for dz, dy in far_first(quarter, WIDTH):
             there = 2 * ((z_first + (z + dz) % quarter) * WIDTH + (y + dy) % WIDTH)
@@ -145,6 +147,11 @@
             if (dz, dy) != (0, 0):
                 yield there + core
 
+    def same_core_peers():
+        for dz, dy in far_first(quarter, WIDTH):
+            if (dz, dy) != (0, 0):
+                yield 2 * ((z_first + (z + dz) % quarter) * WIDTH + (y + dy) % WIDTH) + core
+
     def plane_peers():
         for dz, dy in far_first(length, WIDTH):
             if (dz, dy) != (0, 0):
@@ -162,8 +169,12 @@
         pl.semaphore_signal(barrier, 1, device_id={"seq": peer}, device_id_type=MESH)
     for load in facts_in + loads:
         load.start()
-    for peer in other_half_peers():
-        pl.semaphore_signal(barrier, 1, device_id={"seq": peer}, device_id_type=MESH)
+
+    @pl.when(early)
+    def _():
+        for peer in other_half_peers():
+            pl.semaphore_signal(barrier, 1, device_id={"seq": peer}, device_id_type=MESH)
+
     for step in range(1, heads):
         across = (x + step) % heads
         for seq in (me, other):
@@ -175,7 +186,14 @@
     query = q_ref[...].astype(jnp.float32)
     rows = [query[:, h * HEAD_DIM : (h + 1) * HEAD_DIM] for h in range(16)]
     q_all[off] = jnp.concatenate(rows, axis=0).astype(jnp.bfloat16)
-    pl.semaphore_wait(barrier, (BLOCK - 1) + BLOCK // 2 + 2 * (heads - 1))
+    @pl.when(early)
+    def _():
+        pl.semaphore_wait(barrier, (BLOCK - 1) + 2 * (heads - 1))
+
+    @pl.when(jnp.logical_not(early))
+    def _():
+        pl.semaphore_wait(barrier, (BLOCK - 1) + BLOCK // 2 + 2 * (heads - 1))
+
 
     for peer in block_peers():
         pltpu.make_async_remote_copy(
@@ -197,6 +215,12 @@
     )
 
     weight_copy.start()
+
+    @pl.when(jnp.logical_not(early))
+    def _():
+        for peer in other_half_peers():
+            pl.semaphore_signal(late_sem, 1, device_id={"seq": peer}, device_id_type=MESH)
+
     for load in facts_in:
         load.wait()
     my_start = jnp.int32(0)
@@ -258,7 +282,7 @@
     facts = jnp.where(lane == row, new_top, 0.0) + jnp.where(lane == row + 8, total, 0.0)
     gathered[chip, 8:9, :] = jnp.sum(facts, axis=0, keepdims=True)
 
-    for peer in plane_peers():
+    def send_gathered(peer):
         pltpu.make_async_remote_copy(
             src_ref=gathered.at[chip, pl.ds(0, 9)],
             dst_ref=gathered.at[chip, pl.ds(0, 9)],
@@ -267,6 +291,21 @@
             device_id={"seq": peer},
             device_id_type=MESH,
         ).start()
+
+    @pl.when(early)
+    def _():
+        for peer in same_core_peers():
+            send_gathered(peer)
+        pl.semaphore_wait(late_sem, BLOCK // 2)
+        for peer in other_half_peers():
+            send_gathered(peer)
+
+    @pl.when(jnp.logical_not(early))
+    def _():
+        for there in range(BLOCK // 2):
+            send_gathered(2 * there + core)
+        for peer in same_core_peers():
+            send_gathered(peer)
 
     starts = jnp.zeros((8, chips), jnp.int32)
     ends = jnp.zeros((8, chips), jnp.int32)
@@ -316,7 +355,7 @@
     product[0] = jnp.dot(attended, w_vmem[1], preferred_element_type=jnp.float32)
     ours = jnp.dot(attended, w_vmem[0], preferred_element_type=jnp.float32)
     product[1] = ours
-    terms[slot] = ours
+    own_copy = pltpu.make_async_copy(product.at[1], terms.at[slot], load_sem.at[10])
 
     def final(which, seq, across):
         return pltpu.make_async_remote_copy(
@@ -332,6 +371,7 @@
         final(0, other, (x + step) % heads).start()
         final(1, me, (x + step) % heads).start()
     final(0, other, x).start()
+    own_copy.start()
 
     terms_in = terms.at[pl.ds(0, 2 * heads - 1)]
     terms_copy = pltpu.make_async_remote_copy(
@@ -347,10 +387,7 @@
     swap.wait_send()
     gathered_copy.wait_send()
     terms_copy.wait_recv()
-    out = terms[0]
-    for i in range(1, 2 * heads):
-        out = out + terms[i]
-    out_ref[...] = out[:requests].astype(jnp.bfloat16)
+    own_copy.wait()
     terms_copy.wait_send()
 
 
@@ -363,11 +400,11 @@
     hbm = pl.BlockSpec(memory_space=pl.ANY)
     vmem = pl.BlockSpec(memory_space=pltpu.VMEM)
     smem = pl.BlockSpec(memory_space=pltpu.SMEM)
-    return pl.pallas_call(
+    terms = pl.pallas_call(
         kernel,
-        out_shape=jax.ShapeDtypeStruct((requests, columns), jnp.bfloat16),
+        out_shape=jax.ShapeDtypeStruct((2 * heads, 8, columns), jnp.float32),
         in_specs=[hbm, hbm, hbm, hbm, hbm, hbm, hbm, hbm],
-        out_specs=vmem,
+        out_specs=hbm,
         scratch_shapes=[
             pltpu.VMEM(queries.shape, jnp.bfloat16),
             pltpu.SMEM((requests,), jnp.int32),
@@ -383,15 +420,16 @@
             pltpu.VMEM((24, HEAD_DIM), jnp.float32),
             pltpu.VMEM((chips, 16, HEAD_DIM), jnp.float32),
             pltpu.VMEM((2, 8, columns), jnp.float32),
-            pltpu.VMEM((2 * heads, 8, columns), jnp.float32),
-            pltpu.SemaphoreType.DMA((10,)),
+            pltpu.SemaphoreType.DMA((11,)),
             pltpu.SemaphoreType.DMA((5,)),
             pltpu.SemaphoreType.DMA((5,)),
+            pltpu.SemaphoreType.REGULAR,
         ],
         compiler_params=pltpu.CompilerParams(
             collective_id=0, has_side_effects=True, vmem_limit_bytes=56 * 1024 * 1024
         ),
     )(queries, k_cache, v_cache, o_weight, group_size, group_start, cache_len, owner)
+    return jnp.sum(terms, axis=0)[:requests].astype(jnp.bfloat16)
 
 
 def solution(mesh):

time: 31.8 us -> 30.1 us (0.947)
  Pallas kernels: 30.4 us -> 28.6 us
  other arithmetic: 0 us -> 1.35 us
  local copies, waits for them, and re-layouts: 1.26 us -> 0 us
    pallas_call x1, Pallas kernels: 30.4 us -> 28.6 us  [per_device(): pl.pallas_call(kernel, out_shape=jax.ShapeDtypeStruct((2 * heads, 8, colu...]
    reduce_sum x0 -> x1, other arithmetic: none -> 1.35 us  [per_device(): return jnp.sum(terms, axis=0)[:requests].astype(jnp.bfloat16)]
    unnamed x1 -> x0, local copies, waits for them, and re-layouts: 1.26 us -> none
where the time goes in v3:
time: 30.1 us; the launch traced here: 29.9 us
  Pallas kernels  28.6 us (95%)
  other arithmetic  1.35 us (4%)
    pallas_call x1, Pallas kernels, per_device(): pl.pallas_call(kernel, out_shape=jax.ShapeDtypeStruct((2 * heads, 8, colu...  28.6 us
    reduce_sum x1, other arithmetic, per_device(): return jnp.sum(terms, axis=0)[:requests].astype(jnp.bfloat16)  1.35 us

profile of v3, /device:TPU:1, one launch (start us, length us, event | category | flops | bytes accessed | tf_op | source)
XLA Modules:
  0.0 29.9 jit_solution(18017918192284338687)
XLA Ops:
  0.0 28.6 %shard_map.82 = f32[8,8,128]{2,1,0:T(8,128)} custom-call(bf16[1,2048]{1,0:T(2,128)(2,1)} %q_hbm.1, bf16[12288,256]{1,0:T(8,128)(2,1)} %k_hbm.1, bf16[12288,256]{1,0:T(8,128)(2,1)} %v_hbm.1, bf16[2048,128]{1,0:T(8,128)(2,1)} %w_hbm.1, s32[6]{0:T(128)} %size_hbm.1, s32[6]{0:T(128)} %start_hbm.1, s32[6]{0:T(128)} %length_hbm.1, s32[6]{0:T(128)} %owner_hbm.1), custom_call_target="tpu_custom_call" | custom-call | tf_op jit(solution)/shard_map/pallas_call | solution.py:403
  28.6 1.4 %reduce_sum.9 = bf16[8,128]{1,0:T(8,128)(2,1)} reduce(f32[8,8,128]{2,1,0:T(8,128)} %shard_map.82, f32[]{:T(128)} %constant.0.clone.1), dimensions={0}, to_apply=%region_0.0 | reduce | flops 7168 | bytes 34820 | tf_op jit(solution)/shard_map/reduce_sum | solution.py:432

commit v4 on v3

--- a/solution.py
+++ b/solution.py
@@ -134,28 +134,27 @@
     query_in.start()
 
     z, y = chip // WIDTH, chip % WIDTH
-    length = chips // WIDTH
     quarter = BLOCK // (2 * WIDTH)
     z_first = (z // quarter) * quarter
 
     early = me < BLOCK
 
+    z_own = z % quarter
+    z_there = (z_own, z_own + 1 - 2 * (z_own % 2), (z_own + 2) % quarter, quarter - 1 - z_own)
+    block_steps = [(way, dy) for way in range(quarter) for dy in range(WIDTH)]
+    block_steps.sort(key=lambda s: -(s[0] + min(s[1], WIDTH - s[1])))
+
     def block_peers():
-        for dz, dy in far_first(quarter, WIDTH):
-            there = 2 * ((z_first + (z + dz) % quarter) * WIDTH + (y + dy) % WIDTH)
+        for way, dy in block_steps:
+            there = 2 * ((z_first + z_there[way]) * WIDTH + (y + dy) % WIDTH)
             yield there + 1 - core
-            if (dz, dy) != (0, 0):
+            if (way, dy) != (0, 0):
                 yield there + core
 
     def same_core_peers():
-        for dz, dy in far_first(quarter, WIDTH):
-            if (dz, dy) != (0, 0):
-                yield 2 * ((z_first + (z + dz) % quarter) * WIDTH + (y + dy) % WIDTH) + core
-
-    def plane_peers():
-        for dz, dy in far_first(length, WIDTH):
-            if (dz, dy) != (0, 0):
-                yield 2 * (((z + dz) % length) * WIDTH + (y + dy) % WIDTH) + core
+        for way, dy in block_steps:
+            if (way, dy) != (0, 0):
+                yield 2 * ((z_first + z_there[way]) * WIDTH + (y + dy) % WIDTH) + core
 
     other_half = ((me // BLOCK + 1) % 2) * quarter
 
@@ -352,10 +351,6 @@
 
     weight_copy.wait_recv()
     slot = 2 * x + core
-    product[0] = jnp.dot(attended, w_vmem[1], preferred_element_type=jnp.float32)
-    ours = jnp.dot(attended, w_vmem[0], preferred_element_type=jnp.float32)
-    product[1] = ours
-    own_copy = pltpu.make_async_copy(product.at[1], terms.at[slot], load_sem.at[10])
 
     def final(which, seq, across):
         return pltpu.make_async_remote_copy(
@@ -367,10 +362,18 @@
             device_id_type=MESH,
         )
 
-    for step in (2, 1, 3):
-        final(0, other, (x + step) % heads).start()
-        final(1, me, (x + step) % heads).start()
-    final(0, other, x).start()
+    own_copy = pltpu.make_async_copy(product.at[core], terms.at[slot], load_sem.at[10])
+    for to_core in (1, 0):
+        which = (core + to_core) % 2
+        product[to_core] = jnp.dot(
+            attended, w_vmem[which], preferred_element_type=jnp.float32
+        )
+        for across in range(heads):
+
+            @pl.when(jnp.logical_or(across != x, to_core != core))
+            def _():
+                final(to_core, me - core + to_core, across).start()
+
     own_copy.start()
 
     terms_in = terms.at[pl.ds(0, 2 * heads - 1)]

time: 30.1 us -> 29.6 us (0.983)
  Pallas kernels: 28.6 us -> 28.1 us
    pallas_call x1, Pallas kernels: 28.6 us -> 28.1 us  [per_device(): pl.pallas_call(kernel, out_shape=jax.ShapeDtypeStruct((2 * heads, 8, colu...]
where the time goes in v4:
time: 29.6 us; the launch traced here: 29.5 us
  Pallas kernels  28.1 us (95%)
  other arithmetic  1.35 us (5%)
    pallas_call x1, Pallas kernels, per_device(): pl.pallas_call(kernel, out_shape=jax.ShapeDtypeStruct((2 * heads, 8, colu...  28.1 us
    reduce_sum x1, other arithmetic, per_device(): return jnp.sum(terms, axis=0)[:requests].astype(jnp.bfloat16)  1.35 us

profile of v4, /device:TPU:1, one launch (start us, length us, event | category | flops | bytes accessed | tf_op | source)
XLA Modules:
  0.0 29.5 jit_solution(2958407880772999492)
XLA Ops:
  0.0 28.1 %shard_map.82 = f32[8,8,128]{2,1,0:T(8,128)} custom-call(bf16[1,2048]{1,0:T(2,128)(2,1)} %q_hbm.1, bf16[12288,256]{1,0:T(8,128)(2,1)} %k_hbm.1, bf16[12288,256]{1,0:T(8,128)(2,1)} %v_hbm.1, bf16[2048,128]{1,0:T(8,128)(2,1)} %w_hbm.1, s32[6]{0:T(128)} %size_hbm.1, s32[6]{0:T(128)} %start_hbm.1, s32[6]{0:T(128)} %length_hbm.1, s32[6]{0:T(128)} %owner_hbm.1), custom_call_target="tpu_custom_call" | custom-call | tf_op jit(solution)/shard_map/pallas_call | solution.py:406
  28.1 1.4 %reduce_sum.9 = bf16[8,128]{1,0:T(8,128)(2,1)} reduce(f32[8,8,128]{2,1,0:T(8,128)} %shard_map.82, f32[]{:T(128)} %constant.0.clone.1), dimensions={0}, to_apply=%region_0.0 | reduce | flops 7168 | bytes 34820 | tf_op jit(solution)/shard_map/reduce_sum | solution.py:435

commit v5 on v4

--- a/solution.py
+++ b/solution.py
@@ -213,12 +213,6 @@
         device_id_type=MESH,
     )
 
-    weight_copy.start()
-
-    @pl.when(jnp.logical_not(early))
-    def _():
-        for peer in other_half_peers():
-            pl.semaphore_signal(late_sem, 1, device_id={"seq": peer}, device_id_type=MESH)
 
     for load in facts_in:
         load.wait()
@@ -232,6 +226,11 @@
         my_owner = my_owner + jnp.where(inside, owner_ref[r], 0)
     live = my_length - (me - my_start) * slots
 
+    @pl.when(jnp.logical_not(early))
+    def _():
+        for peer in other_half_peers():
+            pl.semaphore_signal(late_sem, 1, device_id={"seq": peer}, device_id_type=MESH)
+
     for turn in range(2):
         loads[turn].wait()
         for first in range(0, slots, TURN):
@@ -239,6 +238,7 @@
             k_turned[turn, :, rows] = k_vmem[turn, rows, :].T
     for load in loads[2:]:
         load.wait()
+    weight_copy.start()
     queries_in = q_all.at[pl.ds(0, BLOCK - 1)]
     queries_copy = pltpu.make_async_remote_copy(
         src_ref=queries_in,
@@ -301,7 +301,7 @@
 
     @pl.when(jnp.logical_not(early))
     def _():
-        for there in range(BLOCK // 2):
+        for there in (0, 1, 3, 2, 4, 8, 5, 7, 6, 9, 11, 10, 12, 13, 15, 14):
             send_gathered(2 * there + core)
         for peer in same_core_peers():
             send_gathered(peer)

time: 29.6 us -> 29.6 us (level)
  no operation moved by 1% of the time
where the time goes in v5:
time: 29.6 us; the launch traced here: 29.5 us
  Pallas kernels  28.1 us (95%)
  other arithmetic  1.35 us (5%)
    pallas_call x1, Pallas kernels, per_device(): pl.pallas_call(kernel, out_shape=jax.ShapeDtypeStruct((2 * heads, 8, colu...  28.1 us
    reduce_sum x1, other arithmetic, per_device(): return jnp.sum(terms, axis=0)[:requests].astype(jnp.bfloat16)  1.35 us

profile of v5, /device:TPU:1, one launch (start us, length us, event | category | flops | bytes accessed | tf_op | source)
XLA Modules:
  0.0 29.5 jit_solution(6492541915304443431)
XLA Ops:
  0.0 28.1 %shard_map.82 = f32[8,8,128]{2,1,0:T(8,128)} custom-call(bf16[1,2048]{1,0:T(2,128)(2,1)} %q_hbm.1, bf16[12288,256]{1,0:T(8,128)(2,1)} %k_hbm.1, bf16[12288,256]{1,0:T(8,128)(2,1)} %v_hbm.1, bf16[2048,128]{1,0:T(8,128)(2,1)} %w_hbm.1, s32[6]{0:T(128)} %size_hbm.1, s32[6]{0:T(128)} %start_hbm.1, s32[6]{0:T(128)} %length_hbm.1, s32[6]{0:T(128)} %owner_hbm.1), custom_call_target="tpu_custom_call" | custom-call | tf_op jit(solution)/shard_map/pallas_call | solution.py:406
  28.1 1.4 %reduce_sum.9 = bf16[8,128]{1,0:T(8,128)(2,1)} reduce(f32[8,8,128]{2,1,0:T(8,128)} %shard_map.82, f32[]{:T(128)} %constant.0.clone.1), dimensions={0}, to_apply=%region_0.0 | reduce | flops 7168 | bytes 34820 | tf_op jit(solution)/shard_map/reduce_sum | solution.py:435
